TPU v7x, 32 devices: a whole 2x2x4 slice. The times are simulated.
32 devices in a mesh: region: 8 (over z, y), rep: 4 (over x, core).
Axes of the slice: x: 2, y: 2, z: 4, core: 2. Of those that a mesh axis runs over, the one named last changes fastest.
Arguments:
- unit_cost: float32 [16, 131072], P(None, ('region', 'rep')), may hold values from -6 to 6
- start_primal: float32 [16, 131072], P(None, ('region', 'rep')), may hold values from 0 to 0.125
- start_dual: float32 [65536], P('region'), may hold values from 0 to 1
- quota_bound: float32 [65536], P('region'), may hold values from 2 to 6
- person_slot: int32 [131072], P(('region', 'rep')), may hold values from 0 to 1023
- cell_lists: int32 [8, 8, 128], P('region'), may hold values from 0 to 511
Outputs:
- primal: float32 [16, 131072], P(None, ('region', 'rep'))
- dual: float32 [65536], P('region')
Inputs may be any that keep to these rules, and one draw needn't show every extreme that they name: person_slot = d * 128 + j names slot j of the person's region's list toward owner block d.
All inputs are finite; a program needn't handle non-finite values.
Results may differ from a plain program's by a relative error of at most 0.0003.
Values sent between devices are 32-bit elements; how exact they have to be, the bound alone decides.
No kernel may reach another device: no remote copies, remote signals or barrier semaphores. Data moves between devices by JAX's collectives and lax.ppermute only.
A program may use at most 64 MiB of HBM per device.

v0:
```python
import jax
import jax.numpy as jnp
from jax import lax
from jax.sharding import PartitionSpec as P

ITERS = 2
BISECT = 30
PRIMAL_STEP = 0.5
DUAL_STEP = 0.25


def project_simplex(values):
    largest = jnp.max(values, axis=0)

    def bisect_once(repeat, bounds):
        low_end, high_end = bounds
        middle = 0.5 * (low_end + high_end)
        mass_sum = jnp.sum(jnp.maximum(values - middle, 0.0), axis=0)
        above = mass_sum > 1.0
        return (jnp.where(above, middle, low_end), jnp.where(above, high_end, middle))

    low_end, high_end = lax.fori_loop(0, BISECT, bisect_once, (largest - 1.0, largest))
    middle = 0.5 * (low_end + high_end)
    return jnp.maximum(values - middle, 0.0)


def local(unit_cost, start_primal, start_dual, quota_bound, person_slot, cell_lists):
    options = unit_cost.shape[0]
    regions = lax.axis_size("region")
    list_len = cell_lists.shape[2]
    groups = quota_bound.shape[0] // options
    slot_count = regions * list_len
    own_lists = cell_lists[0]
    primal = start_primal
    dual = start_dual
    for repeat in range(ITERS):
        dual_rows = dual.reshape(groups, options)
        picked = jnp.take(dual_rows, own_lists.reshape(-1), axis=0).reshape(
            regions, list_len * options
        )
        slot_arrived = lax.all_to_all(picked, "region", split_axis=0, concat_axis=0, tiled=True)
        prices = slot_arrived.reshape(slot_count, options)
        adjoint = jnp.take(prices, person_slot, axis=0).T
        fresh = project_simplex(primal - PRIMAL_STEP * (unit_cost + adjoint))
        partial_rows = jax.ops.segment_sum(
            (2.0 * fresh - primal).T, person_slot, num_segments=slot_count
        )
        partial_rows = partial_rows.reshape(regions, list_len * options)
        summed = lax.psum(partial_rows, "rep")
        arrived = lax.all_to_all(summed, "region", split_axis=0, concat_axis=0, tiled=True)
        block_sum = jax.ops.segment_sum(
            arrived.reshape(slot_count, options), own_lists.reshape(-1), num_segments=groups
        )
        applied = block_sum.reshape(-1)
        dual = jnp.maximum(dual + DUAL_STEP * (applied - quota_bound), 0.0)
        primal = fresh
    return (primal, dual)


def solution(mesh):
    placed = (
        P(None, ("region", "rep")),
        P(None, ("region", "rep")),
        P("region"),
        P("region"),
        P(("region", "rep")),
        P("region", None, None),
    )
    return jax.shard_map(
        local,
        mesh=mesh,
        in_specs=placed,
        out_specs=(P(None, ("region", "rep")), P("region")),
        check_vma=False,
    )
```

profile of v0, /device:TPU:0, one launch (start us, length us, event | category | flops | bytes accessed | tf_op | source)
XLA Modules:
  0.0 246.2 jit_solution(10379357901981070034)
XLA Ops:
  9.5 2.8 %gather_fusion = f32[1024,16]{1,0:T(8,128)S(1)} fusion(f32[512,16]{1,0:T(8,128)S(1)} %reshape.64, s32[1024]{0:T(1024)S(1)} %fusion.29), kind=kCustom, calls=%fused_computation.clone | custom fusion | bytes 135168 | tf_op jit(solution)/shard_map/jit(_take)/gather | solution.py:38
  13.4 7.3 %all-to-all-start = ((f32[8,1,2048]{2,1,0:T(1,128)}), f32[8,1,2048]{2,1,0:T(1,128)S(1)}, u32[]{:S(2)}, u32[]{:S(2)}) async-start(f32[8,1,2048]{2,1,0:T(1,128)} %all_to_all.32), calls=%async_computation | async-start | bytes 131072 | tf_op jit(solution)/shard_map/all_to_all | solution.py:41
  20.7 2.0 copy.23
  22.7 1.9 copy.24
  24.6 2.9 %all-to-all-done = f32[8,1,2048]{2,1,0:T(1,128)S(1)} async-done(((f32[8,1,2048]{2,1,0:T(1,128)}), f32[8,1,2048]{2,1,0:T(1,128)S(1)}, u32[]{:S(2)}, u32[]{:S(2)}) %all-to-all-start) | async-done | bytes 65568 | tf_op jit(solution)/shard_map/all_to_all | solution.py:41
  27.9 14.1 %gather_fusion.1 = f32[4096,16]{1,0:T(8,128)} fusion(f32[1024,16]{1,0:T(8,128)S(1)} %reshape.65, s32[4096]{0:T(1024)S(1)} %fusion.28), kind=kCustom, calls=%fused_computation.1.clone | custom fusion | bytes 540672 | tf_op jit(solution)/shard_map/jit(_take)/gather | solution.py:43
  42.0 3.5 %fusion.32 = (f32[4096]{0:T(1024)S(1)}, f32[16,4096]{0,1:T(8,128)S(1)}) fusion(f32[16,4096]{0,1:T(8,128)} %copy.24, f32[16,4096]{0,1:T(8,128)} %copy.23, f32[4096,16]{1,0:T(8,128)} %gather_fusion.1, pred[4096]{0:T(1024)(128)(4,1)S(1)} %compare_and_fusion), kind=kLoop, calls=%fused_computation.61 | loop fusion | flops 323584 | bytes 1069056 | tf_op jit(solution)/shard_map/reduce_max | solution.py:13
  46.0 4.1 %while.24 = (s32[]{:T(128)}, f32[4096]{0:T(1024)S(1)}, f32[4096]{0:T(1024)S(1)}, f32[16,4096]{1,0:T(8,128)S(1)}, s32[]{:T(128)}) while((s32[]{:T(128)}, f32[4096]{0:T(1024)S(1)}, f32[4096]{0:T(1024)S(1)}, f32[16,4096]{1,0:T(8,128)S(1)}, s32[]{:T(128)}) %tuple.54), condition=%wide.region_3.6_spmd, body=%wide.region_1.0_spmd.sunk | while | flops 229378 | bytes 499773 | solution.py:22
  50.1 24.9 %scatter_custom_fusion = f32[1024,16]{1,0:T(8,128)S(1)} fusion(s32[4096]{0:T(1024)S(1)} %copy-done.4, f32[16,4096]{0,1:T(8,128)} %copy.24, f32[16,4096]{0,1:T(8,128)S(1)} %get-tuple-element.107, f32[]{:T(128)} %constant.48.clone.1, f32[]{:T(128)} %constant.47.clone.1, f32[4096]{0:T(1024)S(1)} %add_multiply_fusion.3), kind=kCustom, calls=%fused_computation.23 | custom fusion | flops 327680 | bytes 4277760 | tf_op jit(solution)/shard_map/scatter-add | solution.py:45
  76.1 29.6 %all-reduce.3.cloned.1.call-done = f32[8,1,2048]{2,0,1:T(8,128)} async-done(((f32[8,1,2048]{2,0,1:T(8,128)}), f32[8,1,2048]{2,0,1:T(8,128)}) %all-reduce.3.cloned.1.call-update) | async-done | bytes 65552 | tf_op jit(solution)/shard_map/psum | solution.py:49
  106.6 12.2 %all_to_all.38 = f32[8,1,2048]{2,1,0:T(1,128)S(1)} all-to-all(f32[8,1,2048]{2,1,0:T(1,128)S(1)} %copy.27), channel_id=1, replica_groups=mesh['region'=8,'rep'=4] {'region'}, dimensions={0} | all-to-all | bytes 131072 | tf_op jit(solution)/shard_map/all_to_all | solution.py:50
  119.2 6.2 %scatter_custom_fusion.1 = f32[512,16]{1,0:T(8,128)S(1)} fusion(s32[1024]{0:T(1024)} %bitcast.23, f32[1024,16]{1,0:T(8,128)S(1)} %reshape.120, f32[]{:T(128)} %constant.47.clone.1), kind=kCustom, calls=%fused_computation.46 | custom fusion | flops 16384 | bytes 33280 | tf_op jit(solution)/shard_map/scatter-add | solution.py:51
  125.7 2.8 %gather_fusion.2 = f32[1024,16]{1,0:T(8,128)S(1)} fusion(f32[512,16]{1,0:T(8,128)S(1)} %reshape.69, s32[1024]{0:T(1024)S(1)} %fusion.29), kind=kCustom, calls=%fused_computation.2.clone | custom fusion | bytes 135168 | tf_op jit(solution)/shard_map/jit(_take)/gather | solution.py:38
  128.9 9.3 %all_to_all.39 = f32[8,1,2048]{2,1,0:T(1,128)S(1)} all-to-all(f32[8,1,2048]{2,1,0:T(1,128)S(1)} %all_to_all.33), channel_id=1, replica_groups=mesh['region'=8,'rep'=4] {'region'}, dimensions={0} | all-to-all | bytes 131072 | tf_op jit(solution)/shard_map/all_to_all | solution.py:41
  138.6 14.1 %gather_fusion.3 = f32[4096,16]{1,0:T(8,128)} fusion(f32[1024,16]{1,0:T(8,128)S(1)} %reshape.70, s32[4096]{0:T(1024)S(1)} %fusion.28), kind=kCustom, calls=%fused_computation.3.clone | custom fusion | bytes 540672 | tf_op jit(solution)/shard_map/jit(_take)/gather | solution.py:43
  152.7 4.9 %fusion.30 = (f32[4096]{0:T(1024)S(1)}, f32[16,4096]{0,1:T(8,128)}) fusion(f32[16,4096]{0,1:T(8,128)} %copy.23, f32[4096,16]{1,0:T(8,128)} %gather_fusion.3, pred[4096]{0:T(1024)(128)(4,1)S(1)} %compare_and_fusion, f32[16,4096]{0,1:T(8,128)S(1)} %get-tuple-element.107, f32[4096]{0:T(1024)S(1)} %add_multiply_fusion.3), kind=kLoop, calls=%fused_computation.60 | loop fusion | flops 454656 | bytes 1085440 | tf_op jit(solution)/shard_map/reduce_max | solution.py:13
  157.6 2.2 copy.30
  159.7 4.1 %while.25 = (s32[]{:T(128)}, f32[4096]{0:T(1024)S(1)}, f32[4096]{0:T(1024)S(1)}, f32[16,4096]{1,0:T(8,128)S(1)}, s32[]{:T(128)}) while((s32[]{:T(128)}, f32[4096]{0:T(1024)S(1)}, f32[4096]{0:T(1024)S(1)}, f32[16,4096]{1,0:T(8,128)S(1)}, s32[]{:T(128)}) %tuple.57), condition=%wide.region_10.13_spmd, body=%wide.region_8.12_spmd.sunk | while | flops 229378 | bytes 499773 | solution.py:22
  163.8 25.5 %scatter_custom_fusion.2 = f32[1024,16]{1,0:T(8,128)S(1)} fusion(s32[4096]{0:T(1024)S(1)} %copy-done.4, f32[16,4096]{0,1:T(8,128)S(1)} %get-tuple-element.107, f32[]{:T(128)} %constant.48.clone.1, f32[]{:T(128)} %constant.47.clone.1, f32[4096]{0:T(1024)S(1)} %add_multiply_fusion.3, f32[16,4096]{0,1:T(8,128)} %get-tuple-element.105, ...), kind=kCustom, calls=%fused_computation.18 | custom fusion | flops 458752 | bytes 4294144 | tf_op jit(solution)/shard_map/scatter-add | solution.py:45
  190.3 27.8 %all-reduce.5.cloned.1.call-done = f32[8,1,2048]{2,0,1:T(8,128)} async-done(((f32[8,1,2048]{2,0,1:T(8,128)}), f32[8,1,2048]{2,0,1:T(8,128)}) %all-reduce.5.cloned.1.call-update) | async-done | bytes 65552 | tf_op jit(solution)/shard_map/psum | solution.py:49
  219.6 5.5 %all-to-all-start.3 = ((f32[8,1,2048]{2,1,0:T(1,128)}), f32[8,1,2048]{2,1,0:T(1,128)S(1)}, u32[]{:S(2)}, u32[]{:S(2)}) async-start(f32[8,1,2048]{2,1,0:T(1,128)} %copy.31), calls=%async_computation.3 | async-start | bytes 131072 | tf_op jit(solution)/shard_map/all_to_all | solution.py:50
  225.1 1.9 subtract_maximum_fusion
  228.3 3.7 %all-to-all-done.3 = f32[8,1,2048]{2,1,0:T(1,128)S(1)} async-done(((f32[8,1,2048]{2,1,0:T(1,128)}), f32[8,1,2048]{2,1,0:T(1,128)S(1)}, u32[]{:S(2)}, u32[]{:S(2)}) %all-to-all-start.3) | async-done | bytes 65568 | tf_op jit(solution)/shard_map/all_to_all | solution.py:50
  232.4 6.2 %scatter_custom_fusion.3 = f32[512,16]{1,0:T(8,128)S(1)} fusion(s32[1024]{0:T(1024)} %bitcast.24, f32[1024,16]{1,0:T(8,128)S(1)} %reshape.136, f32[]{:T(128)} %constant.47.clone.1), kind=kCustom, calls=%fused_computation.44 | custom fusion | flops 16384 | bytes 33280 | tf_op jit(solution)/shard_map/scatter-add | solution.py:51
  (346 shorter events, 17.5 us)
Async XLA Ops:
  9.4 11.3 %copy-start.4 = (s32[4096]{0:T(1024)S(1)}, s32[4096]{0:T(1024)}, u32[]{:S(2)}) copy-start(s32[4096]{0:T(1024)} %param.18) | copy-start | bytes 49156
  9.4 11.3 %copy-start = (f32[16,4096]{1,0:T(8,128)S(1)}, f32[16,4096]{1,0:T(8,128)}, u32[]{:S(2)}) copy-start(f32[16,4096]{1,0:T(8,128)} %param.14) | copy-start | bytes 786436
  12.3 10.4 %copy-start.1 = (f32[16,4096]{1,0:T(8,128)S(1)}, f32[16,4096]{1,0:T(8,128)}, u32[]{:S(2)}) copy-start(f32[16,4096]{1,0:T(8,128)} %param.15) | copy-start | bytes 786436
  13.4 14.2 %all-to-all-start = ((f32[8,1,2048]{2,1,0:T(1,128)}), f32[8,1,2048]{2,1,0:T(1,128)S(1)}, u32[]{:S(2)}, u32[]{:S(2)}) async-start(f32[8,1,2048]{2,1,0:T(1,128)} %all_to_all.32), calls=%async_computation | async-start | bytes 131072 | tf_op jit(solution)/shard_map/all_to_all | solution.py:41
  20.6 85.0 %all-reduce.3.cloned.1.call-start = ((), (), s32[]{:S(2)}) async-start(), calls=%async_computation.4 | async-start | bytes 131072 | tf_op jit(solution)/shard_map/psum | solution.py:49
  75.1 50.4 %copy-start.2 = (f32[8192]{0:T(1024)S(1)}, f32[8192]{0:T(1024)}, u32[]{:S(2)}) copy-start(f32[8192]{0:T(1024)} %param.16) | copy-start | bytes 98308
  75.1 50.4 %copy-start.3 = (f32[8192]{0:T(1024)S(1)}, f32[8192]{0:T(1024)}, u32[]{:S(2)}) copy-start(f32[8192]{0:T(1024)} %param.17) | copy-start | bytes 98308
  76.0 142.0 %all-reduce.5.cloned.1.call-start = ((), (), s32[]{:S(2)}) async-start(), calls=%async_computation.5 | async-start | bytes 131072 | tf_op jit(solution)/shard_map/psum | solution.py:49
  219.6 12.4 %all-to-all-start.3 = ((f32[8,1,2048]{2,1,0:T(1,128)}), f32[8,1,2048]{2,1,0:T(1,128)S(1)}, u32[]{:S(2)}, u32[]{:S(2)}) async-start(f32[8,1,2048]{2,1,0:T(1,128)} %copy.31), calls=%async_computation.3 | async-start | bytes 131072 | tf_op jit(solution)/shard_map/all_to_all | solution.py:50
Sparse Core Ops, SparseCore 0:
  76.2 29.4 all-reduce.2
  190.4 27.6 all-reduce.4
where the time goes:
time: 247 us; the launch traced here: 246 us
  other arithmetic  81.1 us (33%)
  waiting for transfers between devices  64 us (26%)
  local copies, waits for them, and re-layouts  49.3 us (20%)
  blocking collectives  21.5 us (9%)
  between operations  14.3 us (6%)
  starting transfers between devices  12.9 us (5%)
  loops' own time  3.07 us (1%)
    psum x2, waiting for transfers between devices, local(): summed = lax.psum(partial_rows, 'rep')  57.4 us
    scatter-add x2, other arithmetic, local(): jax.ops.segment_sum((2.0 * fresh - primal).T, person_slot, num_segments=s...  50.5 us
    gather x2, local copies, waits for them, and re-layouts, local(): adjoint = jnp.take(prices, person_slot, axis=0).T  28.2 us
    scatter-add x2, other arithmetic, local(): jax.ops.segment_sum(arrived.reshape(slot_count, options), own_lists.resha...  12.4 us
    all_to_all x1, blocking collectives, local(): lax.all_to_all(summed, 'region', split_axis=0, concat_axis=0, tiled=True)  12.2 us
    all_to_all x1, blocking collectives, local(): lax.all_to_all(picked, 'region', split_axis=0, concat_axis=0, tiled=True)  9.29 us
    reduce_max x2, other arithmetic, project_simplex(): largest = jnp.max(values, axis=0)  8.33 us
    all_to_all x1, starting transfers between devices, local(): lax.all_to_all(picked, 'region', split_axis=0, concat_axis=0, tiled=True)  7.28 us
  transfers between devices with their start and end apart: 4, of which 4 were waited for; matrix products, arithmetic and copies ran while one was open for 3% of the time, Pallas kernels for 0%

commit v1 on v0

--- a/solution.py
+++ b/solution.py
@@ -46,7 +46,7 @@
             (2.0 * fresh - primal).T, person_slot, num_segments=slot_count
         )
         partial_rows = partial_rows.reshape(regions, list_len * options)
-        summed = lax.psum(partial_rows, "rep")
+        summed = jnp.sum(lax.all_gather(partial_rows, "rep"), axis=0)
         arrived = lax.all_to_all(summed, "region", split_axis=0, concat_axis=0, tiled=True)
         block_sum = jax.ops.segment_sum(
             arrived.reshape(slot_count, options), own_lists.reshape(-1), num_segments=groups

time: 247 us -> 180 us (0.73)
  waiting for transfers between devices: 64 us -> 6.62 us
  between operations: 14.3 us -> 0.95 us
  blocking collectives: 21.5 us -> 30.6 us
  local copies, waits for them, and re-layouts: 49.3 us -> 46.3 us
    psum x2 -> x0, waiting for transfers between devices: 57.4 us -> none  [local(): summed = lax.psum(partial_rows, 'rep')]
    all_gather x0 -> x2, blocking collectives: none -> 11.6 us  [local(): summed = jnp.sum(lax.all_gather(partial_rows, 'rep'), axis=0)]
    all_to_all x1, blocking collectives: 12.2 us -> 9.71 us  [local(): lax.all_to_all(summed, 'region', split_axis=0, concat_axis=0, tiled=True)]
  transfers between devices with their start and end apart: 4 -> 2, of which waited for: 4 -> 2; matrix products, arithmetic and copies ran while one was open for 3% -> 4% of each run, Pallas kernels for 0% -> 0%
where the time goes in v1:
time: 180 us; the launch traced here: 179 us
  other arithmetic  81.2 us (45%)
  local copies, waits for them, and re-layouts  46.3 us (26%)
  blocking collectives  30.6 us (17%)
  starting transfers between devices  10.6 us (6%)
  waiting for transfers between devices  6.62 us (4%)
  loops' own time  3.07 us (2%)
    scatter-add x2, other arithmetic, local(): jax.ops.segment_sum((2.0 * fresh - primal).T, person_slot, num_segments=s...  50.5 us
    gather x2, local copies, waits for them, and re-layouts, local(): adjoint = jnp.take(prices, person_slot, axis=0).T  28.2 us
    scatter-add x2, other arithmetic, local(): jax.ops.segment_sum(arrived.reshape(slot_count, options), own_lists.resha...  12.4 us
    all_gather x2, blocking collectives, local(): summed = jnp.sum(lax.all_gather(partial_rows, 'rep'), axis=0)  11.6 us
    all_to_all x1, blocking collectives, local(): lax.all_to_all(summed, 'region', split_axis=0, concat_axis=0, tiled=True)  9.71 us
    all_to_all x1, blocking collectives, local(): lax.all_to_all(picked, 'region', split_axis=0, concat_axis=0, tiled=True)  9.29 us
    reduce_max x2, other arithmetic, project_simplex(): largest = jnp.max(values, axis=0)  8.33 us
    all_to_all x1, starting transfers between devices, local(): lax.all_to_all(picked, 'region', split_axis=0, concat_axis=0, tiled=True)  7.28 us
  transfers between devices with their start and end apart: 2, of which 2 were waited for; matrix products, arithmetic and copies ran while one was open for 4% of the time, Pallas kernels for 0%

profile of v1, /device:TPU:0, one launch (start us, length us, event | category | flops | bytes accessed | tf_op | source)
XLA Modules:
  0.0 179.3 jit_solution(13863019633205259745)
XLA Ops:
  2.9 2.8 %gather_fusion = f32[1024,16]{1,0:T(8,128)S(1)} fusion(f32[512,16]{1,0:T(8,128)S(1)} %reshape.58, s32[1024]{0:T(1024)S(1)} %fusion.29), kind=kCustom, calls=%fused_computation.clone | custom fusion | bytes 135168 | tf_op jit(solution)/shard_map/jit(_take)/gather | solution.py:38
  6.8 7.3 %all-to-all-start = ((f32[8,1,2048]{2,1,0:T(1,128)}), f32[8,1,2048]{2,1,0:T(1,128)S(1)}, u32[]{:S(2)}, u32[]{:S(2)}) async-start(f32[8,1,2048]{2,1,0:T(1,128)} %all_to_all.32), calls=%async_computation | async-start | bytes 131072 | tf_op jit(solution)/shard_map/all_to_all | solution.py:41
  14.1 2.0 %copy.23 = f32[16,4096]{0,1:T(8,128)} copy(f32[16,4096]{1,0:T(8,128)S(1)} %copy-done) | data formatting | bytes 524288 | tf_op args[0]
  16.1 1.9 %copy.24 = f32[16,4096]{0,1:T(8,128)} copy(f32[16,4096]{1,0:T(8,128)S(1)} %copy-done.1) | data formatting | bytes 524288 | tf_op args[1]
  18.0 3.0 %all-to-all-done = f32[8,1,2048]{2,1,0:T(1,128)S(1)} async-done(((f32[8,1,2048]{2,1,0:T(1,128)}), f32[8,1,2048]{2,1,0:T(1,128)S(1)}, u32[]{:S(2)}, u32[]{:S(2)}) %all-to-all-start) | async-done | bytes 65568 | tf_op jit(solution)/shard_map/all_to_all | solution.py:41
  21.4 14.1 %gather_fusion.1 = f32[4096,16]{1,0:T(8,128)} fusion(f32[1024,16]{1,0:T(8,128)S(1)} %reshape.59, s32[4096]{0:T(1024)S(1)} %fusion.28), kind=kCustom, calls=%fused_computation.1.clone | custom fusion | bytes 540672 | tf_op jit(solution)/shard_map/jit(_take)/gather | solution.py:43
  35.5 3.5 %fusion.32 = (f32[4096]{0:T(1024)S(1)}, f32[16,4096]{0,1:T(8,128)S(1)}) fusion(f32[16,4096]{0,1:T(8,128)} %copy.24, f32[16,4096]{0,1:T(8,128)} %copy.23, f32[4096,16]{1,0:T(8,128)} %gather_fusion.1, pred[4096]{0:T(1024)(128)(4,1)S(1)} %compare_and_fusion), kind=kLoop, calls=%fused_computation.61 | loop fusion | flops 323584 | bytes 1069056 | tf_op jit(solution)/shard_map/reduce_max | solution.py:13
  39.5 4.1 %while.24 = (s32[]{:T(128)}, f32[4096]{0:T(1024)S(1)}, f32[4096]{0:T(1024)S(1)}, f32[16,4096]{1,0:T(8,128)S(1)}, s32[]{:T(128)}) while((s32[]{:T(128)}, f32[4096]{0:T(1024)S(1)}, f32[4096]{0:T(1024)S(1)}, f32[16,4096]{1,0:T(8,128)S(1)}, s32[]{:T(128)}) %tuple.54), condition=%wide.region_3.6_spmd, body=%wide.region_1.0_spmd.sunk | while | flops 229378 | bytes 499773 | solution.py:22
  43.6 24.9 %scatter_custom_fusion = f32[1024,16]{1,0:T(8,128)S(1)} fusion(s32[4096]{0:T(1024)S(1)} %copy-done.4, f32[16,4096]{0,1:T(8,128)} %copy.24, f32[16,4096]{0,1:T(8,128)S(1)} %get-tuple-element.107, f32[]{:T(128)} %constant.48.clone.1, f32[]{:T(128)} %constant.10.clone.1, f32[4096]{0:T(1024)S(1)} %add_multiply_fusion.3), kind=kCustom, calls=%fused_computation.23 | custom fusion | flops 327680 | bytes 4277760 | tf_op jit(solution)/shard_map/scatter-add | solution.py:45
  68.9 5.8 %all_gather.6 = f32[4,8,2048]{2,1,0:T(8,128)S(1)} all-gather(f32[1,8,2048]{2,1,0:T(8,128)S(1)} %all_gather_reshape.6), channel_id=1, replica_groups=mesh['region'=8,'rep'=4] {'rep'}, dimensions={0}, use_global_device_ids=true | all-gather | bytes 327680 | tf_op jit(solution)/shard_map/all_gather | solution.py:49
  74.7 9.7 %all_to_all.38 = f32[8,1,2048]{2,1,0:T(1,128)S(1)} all-to-all(f32[8,1,2048]{2,1,0:T(1,128)S(1)} %all_to_all.26), channel_id=1, replica_groups=mesh['region'=8,'rep'=4] {'region'}, dimensions={0} | all-to-all | bytes 131072 | tf_op jit(solution)/shard_map/all_to_all | solution.py:50
  84.8 6.2 %scatter_custom_fusion.1 = f32[512,16]{1,0:T(8,128)S(1)} fusion(s32[1024]{0:T(1024)} %bitcast.23, f32[1024,16]{1,0:T(8,128)S(1)} %reshape.110, f32[]{:T(128)} %constant.10.clone.1), kind=kCustom, calls=%fused_computation.46 | custom fusion | flops 16384 | bytes 33280 | tf_op jit(solution)/shard_map/scatter-add | solution.py:51
  91.3 2.8 %gather_fusion.2 = f32[1024,16]{1,0:T(8,128)S(1)} fusion(f32[512,16]{1,0:T(8,128)S(1)} %reshape.62, s32[1024]{0:T(1024)S(1)} %fusion.29), kind=kCustom, calls=%fused_computation.2.clone | custom fusion | bytes 135168 | tf_op jit(solution)/shard_map/jit(_take)/gather | solution.py:38
  94.6 9.3 %all_to_all.39 = f32[8,1,2048]{2,1,0:T(1,128)S(1)} all-to-all(f32[8,1,2048]{2,1,0:T(1,128)S(1)} %all_to_all.33), channel_id=1, replica_groups=mesh['region'=8,'rep'=4] {'region'}, dimensions={0} | all-to-all | bytes 131072 | tf_op jit(solution)/shard_map/all_to_all | solution.py:41
  104.2 14.1 %gather_fusion.3 = f32[4096,16]{1,0:T(8,128)} fusion(f32[1024,16]{1,0:T(8,128)S(1)} %reshape.63, s32[4096]{0:T(1024)S(1)} %fusion.28), kind=kCustom, calls=%fused_computation.3.clone | custom fusion | bytes 540672 | tf_op jit(solution)/shard_map/jit(_take)/gather | solution.py:43
  118.3 4.9 %fusion.30 = (f32[4096]{0:T(1024)S(1)}, f32[16,4096]{0,1:T(8,128)}) fusion(f32[16,4096]{0,1:T(8,128)} %copy.23, f32[4096,16]{1,0:T(8,128)} %gather_fusion.3, pred[4096]{0:T(1024)(128)(4,1)S(1)} %compare_and_fusion, f32[16,4096]{0,1:T(8,128)S(1)} %get-tuple-element.107, f32[4096]{0:T(1024)S(1)} %add_multiply_fusion.3), kind=kLoop, calls=%fused_computation.60 | loop fusion | flops 454656 | bytes 1085440 | tf_op jit(solution)/shard_map/reduce_max | solution.py:13
  123.2 2.2 %copy.29 = f32[16,4096]{1,0:T(8,128)S(1)} copy(f32[16,4096]{0,1:T(8,128)} %get-tuple-element.105) | data formatting | bytes 524288 | tf_op jit(solution)/shard_map/while | solution.py:22
  125.4 4.1 %while.25 = (s32[]{:T(128)}, f32[4096]{0:T(1024)S(1)}, f32[4096]{0:T(1024)S(1)}, f32[16,4096]{1,0:T(8,128)S(1)}, s32[]{:T(128)}) while((s32[]{:T(128)}, f32[4096]{0:T(1024)S(1)}, f32[4096]{0:T(1024)S(1)}, f32[16,4096]{1,0:T(8,128)S(1)}, s32[]{:T(128)}) %tuple.57), condition=%wide.region_10.13_spmd, body=%wide.region_8.12_spmd.sunk | while | flops 229378 | bytes 499773 | solution.py:22
  129.5 25.5 %scatter_custom_fusion.2 = f32[1024,16]{1,0:T(8,128)S(1)} fusion(s32[4096]{0:T(1024)S(1)} %copy-done.4, f32[16,4096]{0,1:T(8,128)S(1)} %get-tuple-element.107, f32[]{:T(128)} %constant.48.clone.1, f32[]{:T(128)} %constant.10.clone.1, f32[4096]{0:T(1024)S(1)} %add_multiply_fusion.3, f32[16,4096]{0,1:T(8,128)} %get-tuple-element.105, ...), kind=kCustom, calls=%fused_computation.18 | custom fusion | flops 458752 | bytes 4294144 | tf_op jit(solution)/shard_map/scatter-add | solution.py:45
  155.3 5.8 %all_gather.7 = f32[4,8,2048]{2,1,0:T(8,128)S(1)} all-gather(f32[1,8,2048]{2,1,0:T(8,128)S(1)} %all_gather_reshape.7), channel_id=1, replica_groups=mesh['region'=8,'rep'=4] {'rep'}, dimensions={0}, use_global_device_ids=true | all-gather | bytes 327680 | tf_op jit(solution)/shard_map/all_gather | solution.py:49
  161.7 3.3 %all-to-all-start.3 = ((f32[8,1,2048]{2,1,0:T(1,128)}), f32[8,1,2048]{2,1,0:T(1,128)S(1)}, u32[]{:S(2)}, u32[]{:S(2)}) async-start(f32[8,1,2048]{2,1,0:T(1,128)} %all_to_all.30), calls=%async_computation.3 | async-start | bytes 131072 | tf_op jit(solution)/shard_map/all_to_all | solution.py:50
  165.1 1.9 %subtract_maximum_fusion = f32[16,4096]{0,1:T(8,128)S(1)} fusion(f32[16,4096]{0,1:T(8,128)} %get-tuple-element.105, f32[4096]{0:T(1024)S(1)} %add_multiply_fusion.2), kind=kLoop, calls=%fused_computation.30 | loop fusion | flops 131072 | bytes 540672 | tf_op jit(solution)/shard_map/max | solution.py:24
  168.3 3.6 %all-to-all-done.3 = f32[8,1,2048]{2,1,0:T(1,128)S(1)} async-done(((f32[8,1,2048]{2,1,0:T(1,128)}), f32[8,1,2048]{2,1,0:T(1,128)S(1)}, u32[]{:S(2)}, u32[]{:S(2)}) %all-to-all-start.3) | async-done | bytes 65568 | tf_op jit(solution)/shard_map/all_to_all | solution.py:50
  172.3 6.2 %scatter_custom_fusion.3 = f32[512,16]{1,0:T(8,128)S(1)} fusion(s32[1024]{0:T(1024)} %bitcast.24, f32[1024,16]{1,0:T(8,128)S(1)} %reshape.126, f32[]{:T(128)} %constant.10.clone.1), kind=kCustom, calls=%fused_computation.44 | custom fusion | flops 16384 | bytes 33280 | tf_op jit(solution)/shard_map/scatter-add | solution.py:51
  (344 shorter events, 14.5 us)
Async XLA Ops:
  2.9 11.2 %copy-start.4 = (s32[4096]{0:T(1024)S(1)}, s32[4096]{0:T(1024)}, u32[]{:S(2)}) copy-start(s32[4096]{0:T(1024)} %param.18) | copy-start | bytes 49156
  2.9 11.2 %copy-start = (f32[16,4096]{1,0:T(8,128)S(1)}, f32[16,4096]{1,0:T(8,128)}, u32[]{:S(2)}) copy-start(f32[16,4096]{1,0:T(8,128)} %param.14) | copy-start | bytes 786436
  5.7 10.4 %copy-start.1 = (f32[16,4096]{1,0:T(8,128)S(1)}, f32[16,4096]{1,0:T(8,128)}, u32[]{:S(2)}) copy-start(f32[16,4096]{1,0:T(8,128)} %param.15) | copy-start | bytes 786436
  6.8 14.2 %all-to-all-start = ((f32[8,1,2048]{2,1,0:T(1,128)}), f32[8,1,2048]{2,1,0:T(1,128)S(1)}, u32[]{:S(2)}, u32[]{:S(2)}) async-start(f32[8,1,2048]{2,1,0:T(1,128)} %all_to_all.32), calls=%async_computation | async-start | bytes 131072 | tf_op jit(solution)/shard_map/all_to_all | solution.py:41
  68.6 22.6 %copy-start.2 = (f32[8192]{0:T(1024)S(1)}, f32[8192]{0:T(1024)}, u32[]{:S(2)}) copy-start(f32[8192]{0:T(1024)} %param.16) | copy-start | bytes 98308
  68.6 22.6 %copy-start.3 = (f32[8192]{0:T(1024)S(1)}, f32[8192]{0:T(1024)}, u32[]{:S(2)}) copy-start(f32[8192]{0:T(1024)} %param.17) | copy-start | bytes 98308
  161.7 10.2 %all-to-all-start.3 = ((f32[8,1,2048]{2,1,0:T(1,128)}), f32[8,1,2048]{2,1,0:T(1,128)S(1)}, u32[]{:S(2)}, u32[]{:S(2)}) async-start(f32[8,1,2048]{2,1,0:T(1,128)} %all_to_all.30), calls=%async_computation.3 | async-start | bytes 131072 | tf_op jit(solution)/shard_map/all_to_all | solution.py:50
